TPU v7x, 32 devices: a whole 2x2x4 slice. The times are simulated.
32 devices in a mesh: ckpt: 8 (over z, core), rows: 4 (over y, x).
Axes of the slice: x: 2, y: 2, z: 4, core: 2. Of those that a mesh axis runs over, the one named last changes fastest.
Arguments:
- deltas: bfloat16 [8, 4096, 14336], P('ckpt', 'rows'), may hold values from -24 to 24
- start_basis: bfloat16 [8, 14336, 64], P('ckpt', 'rows'), may hold values from -6 to 6
- edit_order: int32 [8], replicated, may hold values from 0 to 7, each once
Outputs:
- merged: bfloat16 [4096, 14336], P('rows', 'ckpt')
Inputs may be any that keep to these rules, and one draw needn't show every extreme that they name: `edit_order`: a permutation: each of 0 to 7 appears once.
All inputs are finite; a program needn't handle non-finite values.
Results may differ from a plain program's by a relative error of at most 0.034.
Values may be sent and summed in bfloat16 or wider, within the bound.
No kernel may reach another device: no remote copies, remote signals or barrier semaphores. Data moves between devices by JAX's collectives and lax.ppermute only.
A program may use at most 128 MiB of HBM per device.

v0:
```python
import math

import jax
import jax.numpy as jnp
from jax import lax
from jax.sharding import PartitionSpec as P

RANK = 64
SUB_ITERS = 2
NS_ITERS = 4


def solve_right(raw, lower_factor):
    return lax.linalg.triangular_solve(
        lower_factor, raw, left_side=False, lower=True, transpose_a=True
    ).astype(jnp.bfloat16)


def local_gram(raw):
    return jnp.dot(raw.T, raw, precision=lax.Precision.HIGHEST)


def cross_gram(stacked, own_cols):
    return lax.dot_general(
        stacked, own_cols, (((0,), (0,)), ((), ())), preferred_element_type=jnp.float32
    )


def update_cols(own_cols, stacked, gram_cols, lead_factor, tail_factor):
    product = jnp.dot(stacked.astype(jnp.float32), gram_cols, precision=lax.Precision.HIGHEST)
    return (lead_factor * own_cols.astype(jnp.float32) + tail_factor * product).astype(jnp.bfloat16)


def body(deltas, start_basis, edit_order):
    changes = deltas[0]
    basis_now = start_basis[0]
    local_rows = changes.shape[0]
    left_basis = jnp.zeros((local_rows, RANK), jnp.bfloat16)
    lower_factor = jnp.zeros((RANK, RANK), jnp.float32)
    for sweep in range(SUB_ITERS):
        left_raw = jnp.dot(
            changes,
            lax.all_gather(basis_now, "rows", axis=0, tiled=True),
            preferred_element_type=jnp.float32,
        )
        left_gram = lax.psum(local_gram(left_raw), "rows")
        left_basis = solve_right(left_raw, jnp.linalg.cholesky(left_gram))
        right_raw = lax.psum_scatter(
            lax.dot_general(
                changes, left_basis, (((0,), (0,)), ((), ())), preferred_element_type=jnp.float32
            ).astype(jnp.bfloat16),
            "rows",
            scatter_dimension=0,
            tiled=True,
        ).astype(jnp.float32)
        right_gram = lax.psum(local_gram(right_raw), "rows")
        lower_factor = jnp.linalg.cholesky(right_gram)
        basis_now = solve_right(right_raw, lower_factor)
    ckpt_count = lax.axis_size("ckpt")
    ckpt_index = lax.axis_index("ckpt")
    left_now = left_basis
    right_now = basis_now
    for step in range(NS_ITERS):
        left_all, right_all = (
            lax.all_gather(left_now, "ckpt", axis=1, tiled=True),
            lax.all_gather(right_now, "ckpt", axis=1, tiled=True),
        )
        gram_left = cross_gram(left_all, left_now)
        gram_right = cross_gram(right_all, right_now)
        gram_left, gram_right = (
            lax.psum(gram_left.astype(jnp.bfloat16), "rows").astype(jnp.float32),
            lax.psum(gram_right.astype(jnp.bfloat16), "rows").astype(jnp.float32),
        )
        if step == 0:
            lead_factor = 1.5 / math.sqrt(ckpt_count)
            tail_factor = -0.5 / (ckpt_count * math.sqrt(ckpt_count))
        else:
            lead_factor = 1.5
            tail_factor = -0.5
        left_now = update_cols(left_now, left_all, gram_left, lead_factor, tail_factor)
        right_now = update_cols(right_now, right_all, gram_right, lead_factor, tail_factor)
    position = jnp.sum(jnp.where(jnp.arange(ckpt_count) == ckpt_index, edit_order, 0))
    weight_now = (1 + position).astype(jnp.float32) / ckpt_count
    scaled_left = jnp.dot(
        left_now.astype(jnp.float32), lower_factor * weight_now, precision=lax.Precision.HIGHEST
    ).astype(jnp.bfloat16)
    left_stack = lax.all_gather(scaled_left, "ckpt", axis=1, tiled=True)
    right_whole = lax.all_gather(right_now, "rows", axis=0, tiled=True)
    right_pick = lax.all_to_all(right_whole, "ckpt", split_axis=0, concat_axis=1, tiled=True)
    merged = lax.dot_general(
        left_stack, right_pick, (((1,), (1,)), ((), ())), preferred_element_type=jnp.float32
    )
    return merged.astype(jnp.bfloat16)


def solution(mesh):
    return jax.shard_map(
        body,
        mesh=mesh,
        in_specs=(P("ckpt", "rows", None), P("ckpt", "rows", None), P()),
        out_specs=P("rows", "ckpt"),
        check_vma=False,
    )
```

profile of v0, /device:TPU:0, one launch (start us, length us, event | category | flops | bytes accessed | tf_op | source)
XLA Modules:
  0.0 862.3 jit_solution(4857279738277284107)
XLA Ops:
  7.3 37.8 %all-gather.36.cloned.1.call-done = bf16[1,14336,64]{1,2,0:T(8,128)(2,1)} async-done(((bf16[1,3584,64]{1,2,0:T(8,128)(2,1)}), bf16[1,14336,64]{1,2,0:T(8,128)(2,1)}) %all-gather.36.cloned.1.call-update) | async-done | bytes 1835024 | tf_op jit(solution)/shard_map/all_gather | solution.py:43
  60.3 15.4 %psum.84 = f32[64,64]{0,1:T(8,128)S(1)} all-reduce(f32[64,64]{0,1:T(8,128)S(1)} %fusion.67), channel_id=1, replica_groups=mesh['ckpt'=8,'rows'=4] {'rows'}, use_global_device_ids=true, to_apply=%region_0.0 | all-reduce | flops 4096 | bytes 32768 | tf_op jit(solution)/shard_map/psum | solution.py:46
  88.2 15.8 %fusion.17 = bf16[14336,64]{0,1:T(8,128)(2,1)} fusion(bf16[1024,64]{0,1:T(8,128)(2,1)S(1)} %fusion.35, bf16[1,1024,14336]{2,1,0:T(8,128)(2,1)} %param.8), kind=kOutput, calls=%fused_computation.11 | convolution fusion | flops 1879965696 | bytes 31326208 | tf_op jit(solution)/shard_map/dot_general | solution.py:49
  104.1 33.1 %reduce-scatter.3.cloned.1.call-done = bf16[3584,64]{0,1:T(8,128)(2,1)} async-done(((bf16[14336,64]{0,1:T(8,128)(2,1)}), bf16[3584,64]{0,1:T(8,128)(2,1)}) %reduce-scatter.3.cloned.1.call-update) | async-done | bytes 458768 | tf_op jit(solution)/shard_map/reduce_scatter | solution.py:48
  138.6 15.6 %psum.85 = f32[64,64]{0,1:T(8,128)S(1)} all-reduce(f32[64,64]{0,1:T(8,128)S(1)} %fusion.68), channel_id=1, replica_groups=mesh['ckpt'=8,'rows'=4] {'rows'}, use_global_device_ids=true, to_apply=%region_4.7 | all-reduce | flops 4096 | bytes 32768 | tf_op jit(solution)/shard_map/psum | solution.py:56
  169.1 33.2 %all-gather.14.cloned.1.call-done = bf16[14336,64]{0,1:T(8,128)(2,1)} async-done(((bf16[3584,64]{0,1:T(8,128)(2,1)}), bf16[14336,64]{0,1:T(8,128)(2,1)}) %all-gather.14.cloned.1.call-update) | async-done | bytes 1835024 | tf_op jit(solution)/shard_map/all_gather | solution.py:43
  217.6 15.6 %psum.86 = f32[64,64]{0,1:T(8,128)S(1)} all-reduce(f32[64,64]{0,1:T(8,128)S(1)} %fusion.69), channel_id=1, replica_groups=mesh['ckpt'=8,'rows'=4] {'rows'}, use_global_device_ids=true, to_apply=%region_5.9 | all-reduce | flops 4096 | bytes 32768 | tf_op jit(solution)/shard_map/psum | solution.py:46
  245.8 15.8 %fusion.14 = bf16[14336,64]{0,1:T(8,128)(2,1)} fusion(bf16[1024,64]{0,1:T(8,128)(2,1)S(1)} %fusion.36, bf16[1,1024,14336]{2,1,0:T(8,128)(2,1)} %param.8), kind=kOutput, calls=%fused_computation.10 | convolution fusion | flops 1879965696 | bytes 31326208 | tf_op jit(solution)/shard_map/dot_general | solution.py:49
  262.3 32.5 %reduce-scatter.5.cloned.1.call-done = bf16[3584,64]{0,1:T(8,128)(2,1)} async-done(((bf16[14336,64]{0,1:T(8,128)(2,1)}), bf16[3584,64]{0,1:T(8,128)(2,1)}) %reduce-scatter.5.cloned.1.call-update) | async-done | bytes 458768 | tf_op jit(solution)/shard_map/reduce_scatter | solution.py:48
  296.2 15.3 %psum.91 = f32[64,64]{0,1:T(8,128)S(1)} all-reduce(f32[64,64]{0,1:T(8,128)S(1)} %fusion.70), channel_id=1, replica_groups=mesh['ckpt'=8,'rows'=4] {'rows'}, use_global_device_ids=true, to_apply=%region_11.15 | all-reduce | flops 4096 | bytes 32768 | tf_op jit(solution)/shard_map/psum | solution.py:56
  329.1 40.2 %all-gather.26.cloned.1.call-done = bf16[3584,512]{0,1:T(8,128)(2,1)} async-done(((bf16[3584,64]{0,1:T(8,128)(2,1)}), bf16[3584,512]{0,1:T(8,128)(2,1)}) %all-gather.26.cloned.1.call-update) | async-done | bytes 3670032 | tf_op jit(solution)/shard_map/all_gather | solution.py:66
  373.4 41.0 %all-reduce.15.cloned.1.call-done = (bf16[512,64]{0,1:T(8,128)(2,1)}, bf16[512,64]{0,1:T(8,128)(2,1)}) async-done(((bf16[512,64]{0,1:T(8,128)(2,1)}, bf16[512,64]{0,1:T(8,128)(2,1)}), (bf16[512,64]{0,1:T(8,128)(2,1)}, bf16[512,64]{0,1:T(8,128)(2,1)})) %all-reduce.15.cloned.1.call-update) | async-done | bytes 131088 | tf_op jit(solution)/shard_map/psum | solution.py:71
  420.3 18.3 %all-gather.18.cloned.1.call-done = bf16[1024,512]{0,1:T(8,128)(2,1)} async-done(((bf16[1024,64]{0,1:T(8,128)(2,1)}), bf16[1024,512]{0,1:T(8,128)(2,1)}) %all-gather.18.cloned.1.call-update) | async-done | bytes 1048592 | tf_op jit(solution)/shard_map/all_gather | solution.py:65
  440.9 41.6 %all-gather.28.cloned.1.call-done = bf16[3584,512]{0,1:T(8,128)(2,1)} async-done(((bf16[3584,64]{0,1:T(8,128)(2,1)}), bf16[3584,512]{0,1:T(8,128)(2,1)}) %all-gather.28.cloned.1.call-update) | async-done | bytes 3670032 | tf_op jit(solution)/shard_map/all_gather | solution.py:66
  486.6 41.0 %all-reduce.13.cloned.1.call-done = (bf16[512,64]{0,1:T(8,128)(2,1)}, bf16[512,64]{0,1:T(8,128)(2,1)}) async-done(((bf16[512,64]{0,1:T(8,128)(2,1)}, bf16[512,64]{0,1:T(8,128)(2,1)}), (bf16[512,64]{0,1:T(8,128)(2,1)}, bf16[512,64]{0,1:T(8,128)(2,1)})) %all-reduce.13.cloned.1.call-update) | async-done | bytes 131088 | tf_op jit(solution)/shard_map/psum | solution.py:71
  533.2 18.5 %all-gather.20.cloned.1.call-done = bf16[1024,512]{0,1:T(8,128)(2,1)} async-done(((bf16[1024,64]{0,1:T(8,128)(2,1)}), bf16[1024,512]{0,1:T(8,128)(2,1)}) %all-gather.20.cloned.1.call-update) | async-done | bytes 1048592 | tf_op jit(solution)/shard_map/all_gather | solution.py:65
  554.1 41.4 %all-gather.30.cloned.1.call-done = bf16[3584,512]{0,1:T(8,128)(2,1)} async-done(((bf16[3584,64]{0,1:T(8,128)(2,1)}), bf16[3584,512]{0,1:T(8,128)(2,1)}) %all-gather.30.cloned.1.call-update) | async-done | bytes 3670032 | tf_op jit(solution)/shard_map/all_gather | solution.py:66
  599.5 41.0 %all-reduce.11.cloned.1.call-done = (bf16[512,64]{0,1:T(8,128)(2,1)}, bf16[512,64]{0,1:T(8,128)(2,1)}) async-done(((bf16[512,64]{0,1:T(8,128)(2,1)}, bf16[512,64]{0,1:T(8,128)(2,1)}), (bf16[512,64]{0,1:T(8,128)(2,1)}, bf16[512,64]{0,1:T(8,128)(2,1)})) %all-reduce.11.cloned.1.call-update) | async-done | bytes 131088 | tf_op jit(solution)/shard_map/psum | solution.py:71
  646.1 18.5 %all-gather.22.cloned.1.call-done = bf16[1024,512]{0,1:T(8,128)(2,1)} async-done(((bf16[1024,64]{0,1:T(8,128)(2,1)}), bf16[1024,512]{0,1:T(8,128)(2,1)}) %all-gather.22.cloned.1.call-update) | async-done | bytes 1048592 | tf_op jit(solution)/shard_map/all_gather | solution.py:65
  666.9 41.5 %all-gather.32.cloned.1.call-done = bf16[3584,512]{0,1:T(8,128)(2,1)} async-done(((bf16[3584,64]{0,1:T(8,128)(2,1)}), bf16[3584,512]{0,1:T(8,128)(2,1)}) %all-gather.32.cloned.1.call-update) | async-done | bytes 3670032 | tf_op jit(solution)/shard_map/all_gather | solution.py:66
  712.5 41.0 %all-reduce.9.cloned.1.call-done = (bf16[512,64]{0,1:T(8,128)(2,1)}, bf16[512,64]{0,1:T(8,128)(2,1)}) async-done(((bf16[512,64]{0,1:T(8,128)(2,1)}, bf16[512,64]{0,1:T(8,128)(2,1)}), (bf16[512,64]{0,1:T(8,128)(2,1)}, bf16[512,64]{0,1:T(8,128)(2,1)})) %all-reduce.9.cloned.1.call-update) | async-done | bytes 131088 | tf_op jit(solution)/shard_map/psum | solution.py:71
  757.1 33.3 %all-gather.34.cloned.1.call-done = bf16[14336,64]{0,1:T(8,128)(2,1)} async-done(((bf16[3584,64]{0,1:T(8,128)(2,1)}), bf16[14336,64]{0,1:T(8,128)(2,1)}) %all-gather.34.cloned.1.call-update) | async-done | bytes 1835024 | tf_op jit(solution)/shard_map/all_gather | solution.py:88
  801.4 30.0 %all-gather.24.cloned.1.call-done = bf16[1024,512]{0,1:T(8,128)(2,1)} async-done(((bf16[1024,64]{0,1:T(8,128)(2,1)}), bf16[1024,512]{0,1:T(8,128)(2,1)}) %all-gather.24.cloned.1.call-update) | async-done | bytes 1048592 | tf_op jit(solution)/shard_map/all_gather | solution.py:87
  831.3 18.5 %all-to-all-done = bf16[8,1792,64]{1,2,0:T(8,128)(2,1)S(1)} async-done(((bf16[8,1792,64]{1,2,0:T(8,128)(2,1)}), bf16[8,1792,64]{1,2,0:T(8,128)(2,1)S(1)}, u32[]{:S(2)}, u32[]{:S(2)}) %all-to-all-start) | async-done | bytes 1835040 | tf_op jit(solution)/shard_map/all_to_all | solution.py:89
  (126 shorter events, 151.3 us)
Async XLA Ops:
  6.5 38.5 %all-gather.36.cloned.1.call-start = ((), (), s32[]{:S(2)}) async-start(), calls=%async_computation.16 | async-start | bytes 2293760 | tf_op jit(solution)/shard_map/all_gather | solution.py:43
  7.3 129.9 %reduce-scatter.3.cloned.1.call-start = ((), (), s32[]{:S(2)}) async-start(), calls=%async_computation.3 | async-start | bytes 2293760 | tf_op jit(solution)/shard_map/reduce_scatter | solution.py:48
  104.0 98.3 %all-gather.14.cloned.1.call-start = ((), (), s32[]{:S(2)}) async-start(), calls=%async_computation.4 | async-start | bytes 2293760 | tf_op jit(solution)/shard_map/all_gather | solution.py:43
  169.1 125.7 %reduce-scatter.5.cloned.1.call-start = ((), (), s32[]{:S(2)}) async-start(), calls=%async_computation.9 | async-start | bytes 2293760 | tf_op jit(solution)/shard_map/reduce_scatter | solution.py:48
  261.7 65.0 %all-gather.16.cloned.1.call-start = ((), (), s32[]{:S(2)}) async-start(), calls=%async_computation.5 | async-start | bytes 1179648 | tf_op jit(solution)/shard_map/all_gather | solution.py:65
  262.3 107.1 %all-gather.26.cloned.1.call-start = ((), (), s32[]{:S(2)}) async-start(), calls=%async_computation.11 | async-start | bytes 4128768 | tf_op jit(solution)/shard_map/all_gather | solution.py:66
  326.6 89.7 %copy-start.3 = (bf16[3584,64]{0,1:T(8,128)(2,1)S(1)}, bf16[3584,64]{0,1:T(8,128)(2,1)}, u32[]{:S(2)}) copy-start(bf16[3584,64]{0,1:T(8,128)(2,1)} %fusion.25) | copy-start | bytes 1376260
  326.6 87.8 %all-reduce.15.cloned.1.call-start = ((), (), s32[]{:S(2)}) async-start(), calls=%async_computation.20 | async-start | bytes 262144 | tf_op jit(solution)/shard_map/psum | solution.py:71
  373.3 65.2 %all-gather.18.cloned.1.call-start = ((), (), s32[]{:S(2)}) async-start(), calls=%async_computation.6 | async-start | bytes 1179648 | tf_op jit(solution)/shard_map/all_gather | solution.py:65
  416.3 66.2 %all-gather.28.cloned.1.call-start = ((), (), s32[]{:S(2)}) async-start(), calls=%async_computation.12 | async-start | bytes 4128768 | tf_op jit(solution)/shard_map/all_gather | solution.py:66
  419.9 109.6 %copy-start = (bf16[3584,64]{0,1:T(8,128)(2,1)S(1)}, bf16[3584,64]{0,1:T(8,128)(2,1)}, u32[]{:S(2)}) copy-start(bf16[3584,64]{0,1:T(8,128)(2,1)} %fusion.26) | copy-start | bytes 1376260
  420.0 107.7 %all-reduce.13.cloned.1.call-start = ((), (), s32[]{:S(2)}) async-start(), calls=%async_computation.19 | async-start | bytes 262144 | tf_op jit(solution)/shard_map/psum | solution.py:71
  438.5 89.1 %copy-start.6 = (bf16[1024,512]{0,1:T(8,128)(2,1)S(1)}, bf16[1024,512]{0,1:T(8,128)(2,1)}, u32[]{:S(2)}) copy-start(bf16[1024,512]{0,1:T(8,128)(2,1)} %all-gather.18.cloned.1.call-done) | copy-start | bytes 3145732
  486.5 65.2 %all-gather.20.cloned.1.call-start = ((), (), s32[]{:S(2)}) async-start(), calls=%async_computation.7 | async-start | bytes 1179648 | tf_op jit(solution)/shard_map/all_gather | solution.py:65
  529.4 66.0 %all-gather.30.cloned.1.call-start = ((), (), s32[]{:S(2)}) async-start(), calls=%async_computation.13 | async-start | bytes 4128768 | tf_op jit(solution)/shard_map/all_gather | solution.py:66
  533.1 109.3 %copy-start.1 = (bf16[3584,64]{0,1:T(8,128)(2,1)S(1)}, bf16[3584,64]{0,1:T(8,128)(2,1)}, u32[]{:S(2)}) copy-start(bf16[3584,64]{0,1:T(8,128)(2,1)} %fusion.27) | copy-start | bytes 1376260
  533.1 107.4 %all-reduce.11.cloned.1.call-start = ((), (), s32[]{:S(2)}) async-start(), calls=%async_computation.18 | async-start | bytes 262144 | tf_op jit(solution)/shard_map/psum | solution.py:71
  599.4 65.2 %all-gather.22.cloned.1.call-start = ((), (), s32[]{:S(2)}) async-start(), calls=%async_computation.8 | async-start | bytes 1179648 | tf_op jit(solution)/shard_map/all_gather | solution.py:65
  642.4 66.1 %all-gather.32.cloned.1.call-start = ((), (), s32[]{:S(2)}) async-start(), calls=%async_computation.14 | async-start | bytes 4128768 | tf_op jit(solution)/shard_map/all_gather | solution.py:66
  646.0 107.5 %copy-start.2 = (bf16[3584,64]{0,1:T(8,128)(2,1)S(1)}, bf16[3584,64]{0,1:T(8,128)(2,1)}, u32[]{:S(2)}) copy-start(bf16[3584,64]{0,1:T(8,128)(2,1)} %fusion.28) | copy-start | bytes 1376260
  646.0 107.5 %all-reduce.9.cloned.1.call-start = ((), (), s32[]{:S(2)}) async-start(), calls=%async_computation.17 | async-start | bytes 262144 | tf_op jit(solution)/shard_map/psum | solution.py:71
  712.4 78.0 %all-gather.34.cloned.1.call-start = ((), (), s32[]{:S(2)}) async-start(), calls=%async_computation.15 | async-start | bytes 2293760 | tf_op jit(solution)/shard_map/all_gather | solution.py:88
  793.4 56.5 %all-to-all-start = ((bf16[8,1792,64]{1,2,0:T(8,128)(2,1)}), bf16[8,1792,64]{1,2,0:T(8,128)(2,1)S(1)}, u32[]{:S(2)}, u32[]{:S(2)}) async-start(bf16[8,1792,64]{1,2,0:T(8,128)(2,1)} %bitcast.132), calls=%async_computation.2 | async-start | bytes 3670016 | tf_op jit(solution)/shard_map/all_to_all | solution.py:89
  798.0 33.3 %all-gather.24.cloned.1.call-start = ((), (), s32[]{:S(2)}) async-start(), calls=%async_computation.10 | async-start | bytes 1179648 | tf_op jit(solution)/shard_map/all_gather | solution.py:87
  (10 other events, 349.7 us)
Sparse Core Ops, SparseCore 0:
  9.2 35.8 all-gather.35
  104.2 32.9 reduce-scatter.2
  169.2 33.1 all-gather.13
  261.8 32.9 reduce-scatter.4
  296.3 22.2 all-gather.15
  326.8 42.5 all-gather.25
  373.5 40.9 all-reduce.14
  416.4 22.0 all-gather.17
  440.3 42.2 all-gather.27
  486.6 40.9 all-reduce.12
  529.6 22.0 all-gather.19
  553.2 42.2 all-gather.29
  599.6 40.9 all-reduce.10
  642.5 22.0 all-gather.21
  666.2 42.2 all-gather.31
  712.5 40.9 all-reduce.8
  757.3 33.1 all-gather.33
  801.5 29.8 all-gather.23
where the time goes:
time: 871 us; the launch traced here: 862 us
  waiting for transfers between devices  604 us (69%)
  matrix products  123 us (14%)
  blocking collectives  61.9 us (7%)
  other arithmetic  49.1 us (6%)
  between operations  15 us (2%)
    all_gather x4, waiting for transfers between devices, body(): lax.all_gather(right_now, 'ckpt', axis=1, tiled=True)  165 us
    psum x4, waiting for transfers between devices, body(): lax.psum(gram_left.astype(jnp.bfloat16), 'rows').astype(jnp.float32)  164 us
    all_gather x2, waiting for transfers between devices, body(): lax.all_gather(basis_now, 'rows', axis=0, tiled=True)  71 us
    reduce_scatter x2, waiting for transfers between devices, body(): lax.psum_scatter(lax.dot_general(changes, left_basis, (((0,), (0,)), ((),...  65.6 us
    all_gather x4, waiting for transfers between devices, body(): lax.all_gather(left_now, 'ckpt', axis=1, tiled=True)  55.3 us
    all_gather x1, waiting for transfers between devices, body(): right_whole = lax.all_gather(right_now, 'rows', axis=0, tiled=True)  33.3 us
    dot_general x2, matrix products, body(): lax.dot_general(changes, left_basis, (((0,), (0,)), ((), ())), preferred_...  31.6 us
    psum x2, blocking collectives, body(): left_gram = lax.psum(local_gram(left_raw), 'rows')  31 us
  transfers between devices with their start and end apart: 19, of which 18 were waited for; matrix products, arithmetic and copies ran while one was open for 5% of the time, Pallas kernels for 0%

commit v1 on v0

v1 whole, which is shorter than its diff:
```python
import functools
import math

import jax
import jax.numpy as jnp
from jax import lax
from jax.experimental import pallas as pl
from jax.experimental.pallas import tpu as pltpu
from jax.sharding import PartitionSpec as P

NS_ITERS = 4
LIFT = 2.0**40
VMEM_BYTES = 56 * 1024 * 1024
HIGH = lax.Precision.HIGHEST


def sweep_kernel(pieces, lift, delta_ref, basis_ref, left_ref, right_ref, total):
    step = pl.program_id(0)
    width = basis_ref.shape[2]
    part = None
    for piece in range(basis_ref.shape[0]):
        term = lax.dot_general(
            delta_ref[:, piece * width:(piece + 1) * width],
            basis_ref[piece],
            (((1,), (1,)), ((), ())),
            preferred_element_type=jnp.float32,
        )
        part = term if part is None else part + term
    left = (jnp.transpose(part) * lift).astype(jnp.bfloat16)
    left_ref[...] = left

    @pl.when(step == 0)
    def _():
        total[...] = jnp.zeros_like(total)

    chunk = pieces[0][1]
    for start, size, _ in pieces:
        total[:, start:start + size] += lax.dot_general(
            left,
            delta_ref[:, start:start + size],
            (((1,), (0,)), ((), ())),
            preferred_element_type=jnp.float32,
        )

    @pl.when(step == pl.num_programs(0) - 1)
    def _():
        for start, size, (group, offset) in pieces:
            right_ref[group, :, offset:offset + size] = total[:, start:start + size].astype(jnp.bfloat16)


def sweep(changes, basis, lift, groups, padded):
    rows, cols = changes.shape
    rank = basis.shape[1]
    real = cols // groups
    block = min(256, rows)
    pieces = []
    for group in range(groups):
        offset = 0
        while offset < real:
            size = min(1792, real - offset)
            pieces.append((group * real + offset, size, (group, offset)))
            offset += size
    return pl.pallas_call(
        functools.partial(sweep_kernel, tuple(pieces), lift),
        grid=(rows // block,),
        in_specs=[
            pl.BlockSpec((block, cols), lambda i: (i, 0)),
            pl.BlockSpec(basis.shape, lambda i: (0, 0, 0)),
        ],
        out_specs=[
            pl.BlockSpec((rank, block), lambda i: (0, i)),
            pl.BlockSpec((groups, rank, padded), lambda i: (0, 0, 0)),
        ],
        out_shape=[
            jax.ShapeDtypeStruct((rank, rows), jnp.bfloat16),
            jax.ShapeDtypeStruct((groups, rank, padded), jnp.bfloat16),
        ],
        scratch_shapes=[pltpu.VMEM((rank, cols), jnp.float32)],
        compiler_params=pltpu.CompilerParams(vmem_limit_bytes=VMEM_BYTES),
        name="sweep",
    )(changes, basis)


def spread(own, axis):
    count = lax.axis_size(axis)
    index = lax.axis_index(axis)
    parts = [own]
    for gap in range(1, count):
        parts.append(lax.ppermute(own, axis, [(src, src ^ gap) for src in range(count)]))
    stacked = jnp.stack(parts)
    order = jnp.arange(count) ^ index
    return jnp.take(stacked, order, axis=0)


def collect(parts, axis):
    count = lax.axis_size(axis)
    index = lax.axis_index(axis)
    total = lax.dynamic_index_in_dim(parts, index, keepdims=False).astype(jnp.float32)
    for gap in range(1, count):
        leaving = lax.dynamic_index_in_dim(parts, index ^ gap, keepdims=False)
        total += lax.ppermute(leaving, axis, [(src, src ^ gap) for src in range(count)]).astype(jnp.float32)
    return total


def inverse_factor(grams):
    lower = jnp.linalg.cholesky(grams)
    unit = jnp.broadcast_to(jnp.eye(grams.shape[-1], dtype=jnp.float32), grams.shape)
    return lax.linalg.triangular_solve(lower, unit, left_side=False, lower=True, transpose_a=True)


def block_diagonal(blocks):
    count, rank, _ = blocks.shape
    unit = jnp.eye(count, dtype=blocks.dtype)
    return (unit[:, None, :, None] * blocks[:, :, None, :]).reshape(count * rank, count * rank)


def own_blocks(gram, count, rank):
    return jnp.stack([gram[c * rank:(c + 1) * rank, c * rank:(c + 1) * rank] for c in range(count)])


def mul(a, b):
    return jnp.dot(a, b, precision=HIGH)


def halves(x):
    high = x.astype(jnp.bfloat16)
    return high, (x - high.astype(jnp.float32)).astype(jnp.bfloat16)


def whiten_kernel(count, gram_ref, diag_ref, out_ref, gram, factor, spare, high, low):
    size = gram_ref.shape[0]
    strip = min(256, size)

    def product(a_ref, b_ref, c_ref, transposed=False, lead=0.0, tail=1.0):
        high[...], low[...] = halves(b_ref[...])
        contract = (((0 if transposed else 1,), (0,)), ((), ()))

        def one(index, _):
            rows = pl.ds(pl.multiple_of(index * strip, strip), strip)
            a = a_ref[:, rows] if transposed else a_ref[rows, :]
            a_high, a_low = halves(a)
            dot = functools.partial(lax.dot_general, dimension_numbers=contract, preferred_element_type=jnp.float32)
            c = tail * (dot(a_high, high[...]) + dot(a_high, low[...]) + dot(a_low, high[...]))
            if not transposed and lead:
                c = c + lead * a
            c_ref[rows, :] = c
            return 0

        lax.fori_loop(0, size // strip, one, 0)

    product(gram_ref, diag_ref, spare)
    product(diag_ref, spare, gram, transposed=True)
    unit = (
        lax.broadcasted_iota(jnp.int32, (size, size), 0) == lax.broadcasted_iota(jnp.int32, (size, size), 1)
    ).astype(jnp.float32)
    lead, tail = 1.5 / math.sqrt(count), -0.5 / (count * math.sqrt(count))
    out_ref[...] = lead * unit + tail * gram[...]

    def one_step(step, _):
        first = step == 1
        lead = jnp.where(first, 1.5 / math.sqrt(count), 1.5)
        tail = jnp.where(first, -0.5 / (count * math.sqrt(count)), -0.5)
        factor[...] = gram[...]
        product_dyn(gram, factor, spare, lead, tail)
        product_dyn(spare, factor, gram, lead, tail)
        factor[...] = gram[...]
        product_dyn(out_ref, factor, spare, 1.5, -0.5)
        out_ref[...] = spare[...]
        return 0

    def product_dyn(a_ref, b_ref, c_ref, lead, tail):
        high[...], low[...] = halves(b_ref[...])

        def one(index, _):
            rows = pl.ds(pl.multiple_of(index * strip, strip), strip)
            a = a_ref[rows, :]
            a_high, a_low = halves(a)
            dot = functools.partial(jnp.dot, preferred_element_type=jnp.float32)
            c = dot(a_high, high[...]) + dot(a_high, low[...]) + dot(a_low, high[...])
            c_ref[rows, :] = lead * a + tail * c
            return 0

        lax.fori_loop(0, size // strip, one, 0)

    lax.fori_loop(1, NS_ITERS, one_step, 0)


def whitener(gram, diag, count):
    size = gram.shape[0]
    return pl.pallas_call(
        functools.partial(whiten_kernel, count),
        out_shape=jax.ShapeDtypeStruct((size, size), jnp.float32),
        scratch_shapes=[pltpu.VMEM((size, size), jnp.float32)] * 3 + [pltpu.VMEM((size, size), jnp.bfloat16)] * 2,
        compiler_params=pltpu.CompilerParams(vmem_limit_bytes=VMEM_BYTES),
        name="whiten",
    )(gram, diag)


def body(deltas, start_basis, edit_order):
    changes = deltas[0]
    start = jnp.transpose(start_basis[0])
    rank = start.shape[0]
    rows_count = lax.axis_size("rows")
    ckpt_count = lax.axis_size("ckpt")
    ckpt_index = lax.axis_index("ckpt")
    cols = changes.shape[1]

    basis = lax.all_gather(start, "rows", axis=0)
    _, right = sweep(changes, basis, LIFT, rows_count, cols // rows_count)
    right = collect(right, "rows").astype(jnp.bfloat16)
    right_all = spread(right, "rows")
    peak = jnp.max(jnp.abs(right_all)).astype(jnp.float32)
    scaled = right_all.astype(jnp.float32) * (1.0 / peak)
    gram = jnp.einsum("nrf,nsf->rs", scaled, scaled, precision=HIGH)
    triangle = inverse_factor(gram[None])[0]
    basis = jnp.einsum("rs,nrf->nsf", triangle, scaled, precision=HIGH).astype(jnp.bfloat16)

    block = cols // ckpt_count
    padded = -(-block // (rows_count * 128)) * 128
    left, right = sweep(changes, basis, 1.0, ckpt_count, padded * rows_count)
    inside = jnp.arange(padded * rows_count) < block
    right = jnp.where(inside, right, 0)
    right = right.reshape(ckpt_count, rank, rows_count, padded).transpose(2, 0, 1, 3)
    right = collect(right, "rows").astype(jnp.bfloat16)
    left_all = lax.all_gather(left, "ckpt", axis=0, tiled=True)
    right = lax.all_to_all(right, "ckpt", split_axis=0, concat_axis=0, tiled=True)
    right = right.reshape(ckpt_count * rank, padded)
    right_all = lax.all_gather(right, "rows", axis=0)

    nt = (((1,), (1,)), ((), ()))
    gram_left = lax.psum(
        lax.dot_general(left_all, left_all, nt, preferred_element_type=jnp.float32), "rows"
    )
    left_t = inverse_factor(own_blocks(gram_left, ckpt_count, rank))
    left_diag = block_diagonal(left_t)
    left_p = whitener(gram_left, left_diag, ckpt_count)

    gram_right = lax.psum(
        lax.dot_general(right, right, nt, preferred_element_type=jnp.float32), ("ckpt", "rows")
    )
    right_own = own_blocks(gram_right, ckpt_count, rank)
    right_t = inverse_factor(right_own)
    right_diag = block_diagonal(right_t)
    right_p = whitener(gram_right, right_diag, ckpt_count)

    weight = (1 + edit_order).astype(jnp.float32) / ckpt_count
    middle = jnp.einsum("crs,crt,ctu->csu", left_t, right_own, right_t, precision=HIGH)
    middle = block_diagonal(middle * weight[:, None, None])
    left_mix = mul(mul(left_diag, left_p), middle)
    right_mix = mul(right_p, right_diag.T)
    mixed = jnp.dot(left_all.T, mul(left_mix, right_mix).astype(jnp.bfloat16), preferred_element_type=jnp.float32)
    merged = jnp.einsum(
        "dk,nkf->dnf", mixed.astype(jnp.bfloat16), right_all, preferred_element_type=jnp.float32
    )
    merged = merged.reshape(merged.shape[0], -1)[:, :block]
    return merged.astype(jnp.bfloat16)


def solution(mesh):
    return jax.shard_map(
        body,
        mesh=mesh,
        in_specs=(P("ckpt", "rows", None), P("ckpt", "rows", None), P()),
        out_specs=P("rows", "ckpt"),
        check_vma=False,
    )
```

time: 871 us -> 636 us (0.73)
  waiting for transfers between devices: 604 us -> 222 us
  other arithmetic: 49.1 us -> 197 us
  matrix products: 123 us -> 32 us
  Pallas kernels: 0 us -> 88.6 us
  blocking collectives: 61.9 us -> 19.8 us
  local copies, waits for them, and re-layouts: 3.31 us -> 41.3 us
    all_gather x12 -> x3, waiting for transfers between devices: 354 us -> 37.8 us  [the longest x1 37.8 us: body(): basis = lax.all_gather(start, 'rows', axis=0)]
    another operation x20 -> x14, other arithmetic: 48.4 us -> 185 us  [the longest x7 101 us: inverse_factor(): lower = jnp.linalg.cholesky(grams)]
    pallas_call x0 -> x4, Pallas kernels: none -> 88.6 us  [the longest x2 52.5 us: sweep(): pl.pallas_call(functools.partial(sweep_kernel, tuple(pieces), lift), grid...]
    dot_general x26 -> x11, matrix products: 117 us -> 30.6 us  [the longest x4 7.4 us: mul(): return jnp.dot(a, b, precision=HIGH)]
    reduce_scatter x2 -> x0, waiting for transfers between devices: 65.6 us -> none  [body(): lax.psum_scatter(lax.dot_general(changes, left_basis, (((0,), (0,)), ((),...]
    psum x4 -> x0, blocking collectives: 61.9 us -> none  [the longest x2 31 us: body(): left_gram = lax.psum(local_gram(left_raw), 'rows')]
    ppermute x0 -> x9, waiting for transfers between devices: none -> 57.7 us  [the longest x6 39.1 us: collect(): lax.ppermute(leaving, axis, [(src, src ^ gap) for src in range(count)])]
    psum x4 -> x2, waiting for transfers between devices: 164 us -> 125 us  [the longest x1 124 us: body(): lax.psum(lax.dot_general(right, right, nt, preferred_element_type=jnp.flo...]
  transfers between devices with their start and end apart: 19 -> 14, of which waited for: 18 -> 9; matrix products, arithmetic and copies ran while one was open for 5% -> 34% of each run, Pallas kernels for 0% -> 6%
where the time goes in v1:
time: 636 us; the launch traced here: 626 us
  waiting for transfers between devices  222 us (35%)
  other arithmetic  197 us (31%)
  Pallas kernels  88.6 us (14%)
  local copies, waits for them, and re-layouts  41.3 us (6%)
  matrix products  32 us (5%)
  blocking collectives  19.8 us (3%)
  between operations  14.6 us (2%)
  starting transfers between devices  11 us (2%)
    psum x1, waiting for transfers between devices, body(): lax.psum(lax.dot_general(right, right, nt, preferred_element_type=jnp.flo...  124 us
    another operation x7, other arithmetic, inverse_factor(): lower = jnp.linalg.cholesky(grams)  101 us
    another operation x6, other arithmetic, inverse_factor(): lax.linalg.triangular_solve(lower, unit, left_side=False, lower=True, tra...  84.3 us
    pallas_call x2, Pallas kernels, sweep(): pl.pallas_call(functools.partial(sweep_kernel, tuple(pieces), lift), grid...  52.5 us
    ppermute x6, waiting for transfers between devices, collect(): lax.ppermute(leaving, axis, [(src, src ^ gap) for src in range(count)])  39.1 us
    all_gather x1, waiting for transfers between devices, body(): basis = lax.all_gather(start, 'rows', axis=0)  37.8 us
    pallas_call x2, Pallas kernels, whitener(): pl.pallas_call(functools.partial(whiten_kernel, count), out_shape=jax.Sha...  36.1 us
    all_to_all x1, blocking collectives, body(): lax.all_to_all(right, 'ckpt', split_axis=0, concat_axis=0, tiled=True)  19.8 us
  transfers between devices with their start and end apart: 14, of which 9 were waited for; matrix products, arithmetic and copies ran while one was open for 34% of the time, Pallas kernels for 6%

profile of v1, /device:TPU:0, one launch (start us, length us, event | category | flops | bytes accessed | tf_op | source)
XLA Modules:
  0.0 626.0 jit_solution(7855399479053683755)
XLA Ops:
  7.3 37.8 %all-gather.9.cloned.1.call-done = bf16[256,3584]{1,0:T(8,128)(2,1)} async-done(((bf16[64,3584]{1,0:T(8,128)(2,1)}), bf16[256,3584]{1,0:T(8,128)(2,1)}) %all-gather.9.cloned.1.call-update) | async-done | bytes 1835024 | tf_op jit(solution)/shard_map/all_gather | solution.py:208
  45.1 26.2 %sweep.2 = (bf16[64,1024]{1,0:T(8,128)(2,1)}, bf16[4,64,3584]{2,1,0:T(8,128)(2,1)}) custom-call(bf16[1024,14336]{1,0:T(8,128)(2,1)} %bitcast.169, bf16[4,64,3584]{2,1,0:T(8,128)(2,1)} %bitcast.175), custom_call_target="tpu_custom_call" | custom-call | tf_op jit(solution)/shard_map/sweep/pallas_call | solution.py:63
  76.2 9.9 %collective-permute-done = bf16[64,3584]{1,0:T(8,128)(2,1)S(1)} collective-permute-done((bf16[64,3584]{1,0:T(8,128)(2,1)S(1)}, bf16[64,3584]{1,0:T(8,128)(2,1)S(1)}, u32[]{:S(2)}, u32[]{:S(2)}) %collective-permute-start) | collective-permute-done | bytes 458784 | tf_op jit(solution)/shard_map/ppermute | solution.py:101
  86.2 9.9 %collective-permute-done.1 = bf16[64,3584]{1,0:T(8,128)(2,1)S(1)} collective-permute-done((bf16[64,3584]{1,0:T(8,128)(2,1)S(1)}, bf16[64,3584]{1,0:T(8,128)(2,1)S(1)}, u32[]{:S(2)}, u32[]{:S(2)}) %collective-permute-start.1) | collective-permute-done | bytes 458784 | tf_op jit(solution)/shard_map/ppermute | solution.py:101
  100.9 17.4 %collective-permute-done.4 = bf16[64,3584]{1,0:T(8,128)(2,1)S(1)} collective-permute-done((bf16[64,3584]{1,0:T(8,128)(2,1)S(1)}, bf16[64,3584]{1,0:T(8,128)(2,1)S(1)}, u32[]{:S(2)}, u32[]{:S(2)}) %collective-permute-start.4) | collective-permute-done | bytes 458784 | tf_op jit(solution)/shard_map/ppermute | solution.py:89
  125.0 6.0 fusion.1
  131.1 5.8 custom-call.13
  138.2 4.9 custom-call.14
  143.3 5.2 fusion.basis_ref
  148.5 26.3 %sweep.3 = (bf16[64,1024]{1,0:T(8,128)(2,1)}, bf16[8,64,2048]{2,1,0:T(8,128)(2,1)}) custom-call(bf16[1024,14336]{1,0:T(8,128)(2,1)} %bitcast.170, bf16[4,64,3584]{2,1,0:T(8,128)(2,1)} %fusion.basis_ref), custom_call_target="tpu_custom_call" | custom-call | tf_op jit(solution)/shard_map/sweep/pallas_call | solution.py:63
  181.2 4.7 constant_dynamic-slice_fusion.3
  190.1 10.9 %collective-permute-done.6 = bf16[8,64,512]{2,1,0:T(8,128)(2,1)S(1)} collective-permute-done((bf16[8,64,512]{2,1,0:T(8,128)(2,1)S(1)}, bf16[8,64,512]{2,1,0:T(8,128)(2,1)S(1)}, u32[]{:S(2)}, u32[]{:S(2)}) %collective-permute-start.6) | collective-permute-done | bytes 524320 | tf_op jit(solution)/shard_map/ppermute | solution.py:101
  201.0 8.4 %collective-permute-done.7 = bf16[8,64,512]{2,1,0:T(8,128)(2,1)} collective-permute-done((bf16[8,64,512]{2,1,0:T(8,128)(2,1)S(1)}, bf16[8,64,512]{2,1,0:T(8,128)(2,1)}, u32[]{:S(2)}, u32[]{:S(2)}) %collective-permute-start.7) | collective-permute-done | bytes 524320 | tf_op jit(solution)/shard_map/ppermute | solution.py:101
  210.9 19.8 %all_to_all.5 = bf16[8,64,512]{2,1,0:T(8,128)(2,1)S(1)} all-to-all(bf16[8,64,512]{2,1,0:T(8,128)(2,1)S(1)} %fusion.7), channel_id=1, replica_groups=mesh['ckpt'=8,'rows'=4] {'ckpt'}, dimensions={0} | all-to-all | bytes 1048576 | tf_op jit(solution)/shard_map/all_to_all | solution.py:226
  236.1 124.0 %all-reduce.5.cloned.1.call-done.gram_ref = f32[512,512]{1,0:T(8,128)} async-done(((f32[512,512]{1,0:T(8,128)}), f32[512,512]{1,0:T(8,128)}) %all-reduce.5.cloned.1.call-update) | async-done | bytes 1048592 | tf_op jit(solution)/shard_map/psum | solution.py:238
  366.7 47.1 %custom-call.19 = f32[8,64,64]{2,1,0:T(8,128)S(1)} custom-call(f32[8,64,64]{2,1,0:T(8,128)S(1)} %copy.69), custom_call_target="Cholesky" | custom-call | tf_op jit(solution)/shard_map/jit(cholesky)/cholesky | solution.py:106
  421.9 46.9 %custom-call.17 = f32[8,64,64]{2,1,0:T(8,128)S(1)} custom-call(f32[8,64,64]{2,1,0:T(8,128)S(1)} %copy.59), custom_call_target="Cholesky" | custom-call | tf_op jit(solution)/shard_map/jit(cholesky)/cholesky | solution.py:106
  469.2 39.3 %custom-call.18 = f32[8,1,64,64]{2,3,1,0:T(8,128)S(1)} custom-call(f32[8,1,64,64]{3,2,1,0:T(8,128)S(1)} %get-tuple-element.23), custom_call_target="InvertDiagBlocksLowerTriangular" | custom-call | tf_op jit(solution)/shard_map/triangular_solve/custom-call.3 | solution.py:108
  508.5 39.3 %custom-call.20 = f32[8,1,64,64]{2,3,1,0:T(8,128)S(1)} custom-call(f32[8,1,64,64]{3,2,1,0:T(8,128)S(1)} %get-tuple-element.22), custom_call_target="InvertDiagBlocksLowerTriangular" | custom-call | tf_op jit(solution)/shard_map/triangular_solve/custom-call.3 | solution.py:108
  559.0 17.8 %whiten.3 = f32[512,512]{1,0:T(8,128)} custom-call(f32[512,512]{1,0:T(8,128)} %all-reduce.5.cloned.1.call-done.gram_ref, f32[512,512]{1,0:T(8,128)} %mul.78.diag_ref), custom_call_target="tpu_custom_call" | custom-call | tf_op jit(solution)/shard_map/whiten/pallas_call | solution.py:190
  576.8 18.2 %whiten.2 = f32[512,512]{1,0:T(8,128)} custom-call(f32[512,512]{1,0:T(8,128)} %all-reduce.3.cloned.1.call-done.gram_ref, f32[512,512]{1,0:T(8,128)} %mul.70.diag_ref), custom_call_target="tpu_custom_call" | custom-call | tf_op jit(solution)/shard_map/whiten/pallas_call | solution.py:190
  602.6 6.4 %convolution_convert_fusion.1 = bf16[1024,4,512]{0,2,1:T(8,128)(2,1)} fusion(bf16[4,512,512]{2,1,0:T(8,128)(2,1)} %all-gather.7.cloned.1.call-done, bf16[512,1024]{1,0:T(8,128)(2,1)S(1)} %copy-done.6, bf16[512,512]{1,0:T(8,128)(2,1)S(1)} %convolution_convert_fusion.3), kind=kOutput, calls=%fused_computation.5 | convolution fusion | flops 2686976000 | bytes 7864320 | tf_op jit(solution)/shard_map/dk,nkf->dnf/dot_general | solution.py:252
  608.9 4.2 slice.103
  613.1 5.9 copy.90
  (109 shorter events, 69.1 us)
Async XLA Ops:
  6.5 38.5 %all-gather.9.cloned.1.call-start = ((), (), s32[]{:S(2)}) async-start(), calls=%async_computation.5 | async-start | bytes 2293760 | tf_op jit(solution)/shard_map/all_gather | solution.py:208
  7.3 224.9 %all-gather.5.cloned.1.call-start = ((), (), s32[]{:S(2)}) async-start(), calls=%async_computation.1 | async-start | bytes 1179648 | tf_op jit(solution)/shard_map/all_gather | solution.py:225
  72.7 13.5 %collective-permute-start = (bf16[64,3584]{1,0:T(8,128)(2,1)S(1)}, bf16[64,3584]{1,0:T(8,128)(2,1)S(1)}, u32[]{:S(2)}, u32[]{:S(2)}) collective-permute-start(bf16[64,3584]{1,0:T(8,128)(2,1)S(1)} %get-tuple-element.19), channel_id=1, source_target_pairs={{0,1},{1,0},{2,3},{3,2},{4,5},{5,4},{6,7},{7,6},{8,9},{9,8},{10,11... | collective-permute-start | bytes 1376264 | tf_op jit(solution)/shard_map/ppermute | solution.py:101
  74.2 21.8 %collective-permute-start.1 = (bf16[64,3584]{1,0:T(8,128)(2,1)S(1)}, bf16[64,3584]{1,0:T(8,128)(2,1)S(1)}, u32[]{:S(2)}, u32[]{:S(2)}) collective-permute-start(bf16[64,3584]{1,0:T(8,128)(2,1)S(1)} %get-tuple-element.21), channel_id=1, source_target_pairs={{0,2},{1,3},{2,0},{3,1},{4,6},{5,7},{6,4},{7,5},{8,10},{9,11},{10,... | collective-permute-start | bytes 1376264 | tf_op jit(solution)/shard_map/ppermute | solution.py:101
  74.8 21.3 %collective-permute-start.2 = (bf16[64,3584]{1,0:T(8,128)(2,1)S(1)}, bf16[64,3584]{1,0:T(8,128)(2,1)S(1)}, u32[]{:S(2)}, u32[]{:S(2)}) collective-permute-start(bf16[64,3584]{1,0:T(8,128)(2,1)S(1)} %get-tuple-element.20), channel_id=1, source_target_pairs={{0,3},{1,2},{2,1},{3,0},{4,7},{5,6},{6,5},{7,4},{8,11},{9,10},{10,... | collective-permute-start | bytes 1376264 | tf_op jit(solution)/shard_map/ppermute | solution.py:101
  97.3 21.0 %collective-permute-start.4 = (bf16[64,3584]{1,0:T(8,128)(2,1)S(1)}, bf16[64,3584]{1,0:T(8,128)(2,1)S(1)}, u32[]{:S(2)}, u32[]{:S(2)}) collective-permute-start(bf16[64,3584]{1,0:T(8,128)(2,1)S(1)} %fusion.10), channel_id=1, source_target_pairs={{0,2},{1,3},{2,0},{3,1},{4,6},{5,7},{6,4},{7,5},{8,10},{9,11},{10,... | collective-permute-start | bytes 1376264 | tf_op jit(solution)/shard_map/ppermute | solution.py:89
  97.9 20.4 %collective-permute-start.5 = (bf16[64,3584]{1,0:T(8,128)(2,1)S(1)}, bf16[64,3584]{1,0:T(8,128)(2,1)S(1)}, u32[]{:S(2)}, u32[]{:S(2)}) collective-permute-start(bf16[64,3584]{1,0:T(8,128)(2,1)S(1)} %fusion.10), channel_id=1, source_target_pairs={{0,3},{1,2},{2,1},{3,0},{4,7},{5,6},{6,5},{7,4},{8,11},{9,10},{10,... | collective-permute-start | bytes 1376264 | tf_op jit(solution)/shard_map/ppermute | solution.py:89
  99.4 20.2 %collective-permute-start.3 = (bf16[64,3584]{1,0:T(8,128)(2,1)S(1)}, bf16[64,3584]{1,0:T(8,128)(2,1)S(1)}, u32[]{:S(2)}, u32[]{:S(2)}) collective-permute-start(bf16[64,3584]{1,0:T(8,128)(2,1)S(1)} %fusion.10), channel_id=1, source_target_pairs={{0,1},{1,0},{2,3},{3,2},{4,5},{5,4},{6,7},{7,6},{8,9},{9,8},{10,11... | collective-permute-start | bytes 1376264 | tf_op jit(solution)/shard_map/ppermute | solution.py:89
  125.0 18.4 %copy-start.3 = (bf16[4,64,3584]{2,1,0:T(8,128)(2,1)S(1)}, bf16[4,64,3584]{2,1,0:T(8,128)(2,1)}, u32[]{:S(2)}) copy-start(bf16[4,64,3584]{2,1,0:T(8,128)(2,1)} %gather_fusion) | copy-start | bytes 5505028
  186.0 14.9 %collective-permute-start.6 = (bf16[8,64,512]{2,1,0:T(8,128)(2,1)S(1)}, bf16[8,64,512]{2,1,0:T(8,128)(2,1)S(1)}, u32[]{:S(2)}, u32[]{:S(2)}) collective-permute-start(bf16[8,64,512]{2,1,0:T(8,128)(2,1)S(1)} %bitcast.176), channel_id=1, source_target_pairs={{0,1},{1,0},{2,3},{3,2},{4,5},{5,4},{6,7},{7,6},{8,9},{9,8},{10,11... | collective-permute-start | bytes 1572872 | tf_op jit(solution)/shard_map/ppermute | solution.py:101
  186.8 22.5 %collective-permute-start.7 = (bf16[8,64,512]{2,1,0:T(8,128)(2,1)S(1)}, bf16[8,64,512]{2,1,0:T(8,128)(2,1)}, u32[]{:S(2)}, u32[]{:S(2)}) collective-permute-start(bf16[8,64,512]{2,1,0:T(8,128)(2,1)S(1)} %bitcast.177), channel_id=1, source_target_pairs={{0,2},{1,3},{2,0},{3,1},{4,6},{5,7},{6,4},{7,5},{8,10},{9,11},{10,... | collective-permute-start | bytes 1572872 | tf_op jit(solution)/shard_map/ppermute | solution.py:101
  188.5 20.9 %collective-permute-start.8 = (bf16[8,64,512]{2,1,0:T(8,128)(2,1)S(1)}, bf16[8,64,512]{2,1,0:T(8,128)(2,1)}, u32[]{:S(2)}, u32[]{:S(2)}) collective-permute-start(bf16[8,64,512]{2,1,0:T(8,128)(2,1)S(1)} %bitcast.178), channel_id=1, source_target_pairs={{0,3},{1,2},{2,1},{3,0},{4,7},{5,6},{6,5},{7,4},{8,11},{9,10},{10,... | collective-permute-start | bytes 1572872 | tf_op jit(solution)/shard_map/ppermute | solution.py:101
  190.0 170.0 %all-reduce.5.cloned.1.call-start = ((), (), s32[]{:S(2)}) async-start(), calls=%async_computation.3 | async-start | bytes 2097152 | tf_op jit(solution)/shard_map/psum | solution.py:238
  230.6 4.8 copy-start.2
  232.1 3.5 copy-start.7
  232.1 183.1 %all-reduce.3.cloned.1.call-start = ((), (), s32[]{:S(2)}) async-start(), calls=%async_computation.2 | async-start | bytes 2097152 | tf_op jit(solution)/shard_map/psum | solution.py:231
  235.5 367.1 %all-gather.7.cloned.1.call-start = ((), (), s32[]{:S(2)}) async-start(), calls=%async_computation.4 | async-start | bytes 2621440 | tf_op jit(solution)/shard_map/all_gather | solution.py:228
  576.8 18.3 %copy-start.1 = (f32[512,512]{1,0:T(8,128)S(1)}, f32[512,512]{1,0:T(8,128)}, u32[]{:S(2)}) copy-start(f32[512,512]{1,0:T(8,128)} %mul.78.diag_ref) | copy-start | bytes 3145732
  576.8 18.3 %copy-start.5 = (f32[512,512]{1,0:T(8,128)S(1)}, f32[512,512]{1,0:T(8,128)}, u32[]{:S(2)}) copy-start(f32[512,512]{1,0:T(8,128)} %whiten.3) | copy-start | bytes 3145732
  595.0 1.9 copy-start
  595.1 1.9 copy-start.4
  600.7 1.9 copy-start.6
Sparse Core Ops, SparseCore 0:
  9.2 35.8 all-gather.8
  190.1 21.8 all-gather.4
  232.2 127.7 all-reduce.4
  363.2 51.9 all-reduce.2
  417.1 35.7 all-gather.6
